TPU v7x, 32 devices: a whole 2x2x4 slice. The times are simulated.
32 devices in a mesh: tm: 2 (over y), freq: 4 (over z), dish: 4 (over x, core).
Axes of the slice: x: 2, y: 2, z: 4, core: 2. Of those that a mesh axis runs over, the one named last changes fastest.
Arguments:
- time_data: bfloat16 [64, 512, 1024], P('dish', 'freq', 'tm'), may hold values from -24 to 24
- pointing: bfloat16 [8, 128, 128], P('tm'), may hold values from -0.5 to 0.5
- coverage: int32 [8], P('tm'), may hold values from 0 to 15
- noise_inv: bfloat16 [64, 128, 128], P('dish'), as said below
- gains: float32 [64, 512, 8], P('dish', 'freq', 'tm'), may hold values from 0.1 to 1.9
- prior_inv: float32 [512, 512], replicated, as said below
- precond: float32 [512, 2048], P('freq', ('tm', 'dish')), may hold values from 0.5 to 200
Outputs:
- map_estimate: float32 [512, 2048], P('freq', ('tm', 'dish'))
- residual: float32 [512, 2048], P('freq', ('tm', 'dish'))
Inputs may be any that keep to these rules, and one draw needn't show every extreme that they name: `noise_inv`: each matrix is symmetric with a positive diagonal that dominates its row, and zero where two samples lie more than 16 apart. `prior_inv`: symmetric with a positive diagonal that dominates its row.
All inputs are finite; a program needn't handle non-finite values.
Results may differ from a plain program's by a relative error of at most 0.0045.
Values may be sent and summed in bfloat16 or wider, within the bound.
A program may use at most 64 MiB of HBM per device.

v0:
```python
import functools

import jax
import jax.numpy as jnp
from jax import lax
from jax.experimental import pallas as pl
from jax.experimental.pallas import tpu as pltpu
from jax.sharding import PartitionSpec as P

ITERS = 4
BAND = 16
DIAGS = 2 * BAND + 1
ROWS = 16
LANES = 128
MESH = pl.DeviceIdType.MESH


def shifted(block, axis, distance):
    devices = range(lax.axis_size(axis))
    route = [((i - distance) % len(devices), i) for i in devices]
    return lax.ppermute(block, axis, route)


def general_body(time_data, pointing, coverage, noise_inv, gains, prior_inv, precond):
    highest = lax.Precision.HIGHEST
    channels_dev = precond.shape[0]
    owned_pixels = precond.shape[1]
    blocks_dev = pointing.shape[0]
    dish_count = lax.axis_size("dish")
    owned_tiles = owned_pixels // 128
    region_tiles = owned_tiles * dish_count
    window_tiles = 2 * region_tiles
    tile_count = jnp.arange(owned_tiles, dtype=jnp.int32)
    first_owned = lax.axis_index("dish") * owned_tiles + tile_count
    wanted = jnp.concatenate([first_owned, first_owned + region_tiles])
    own_hot = (coverage[:, None] == wanted[None, :]).astype(jnp.float32)

    def collect(partial_tod):
        summed = lax.psum(partial_tod, "dish")
        tile_part = jnp.einsum(
            "cbt,bti->cbi",
            summed.astype(jnp.bfloat16),
            pointing,
            preferred_element_type=jnp.float32,
        )
        window = jnp.einsum("cbi,bw->cwi", tile_part, own_hot, precision=highest)
        own_part = window[:, :owned_tiles, :].reshape(channels_dev, owned_pixels)
        ahead_part = window[:, owned_tiles:, :].reshape(channels_dev, owned_pixels)
        arrived = shifted(ahead_part, "tm", 1)
        return own_part + arrived

    def energy_of(residual, scaled):
        return lax.psum(jnp.sum(residual * scaled), ("tm", "freq", "dish"))

    series = time_data.reshape(time_data.shape[0], channels_dev, blocks_dev, 128)
    rhs_weighted = jnp.einsum(
        "dcbs,dst->dcbt", series, noise_inv, preferred_element_type=jnp.float32
    )
    right_side = collect(jnp.sum(gains[:, :, :, None] * rhs_weighted, axis=0))
    estimate = jnp.zeros_like(right_side)
    residual = right_side
    scaled = precond * residual
    direction = scaled
    energy_now = energy_of(residual, scaled)
    for iteration in range(ITERS):
        swapped = lax.all_to_all(direction, "freq", split_axis=1, concat_axis=0, tiled=True)
        applied = jnp.dot(prior_inv, swapped, precision=highest, preferred_element_type=jnp.float32)
        region_map = lax.all_gather(direction.astype(jnp.bfloat16), "dish", axis=1, tiled=True)
        following = shifted(region_map, "tm", -1)
        data_window = jnp.concatenate([region_map, following], axis=1)
        tile_maps = data_window.reshape(channels_dev, window_tiles, 128)[:, coverage, :]
        model_tod = jnp.einsum(
            "cbp,bsp->cbs", tile_maps, pointing, preferred_element_type=jnp.float32
        ).astype(jnp.bfloat16)
        weighted = jnp.einsum(
            "cbs,dst->dcbt", model_tod, noise_inv, preferred_element_type=jnp.float32
        )
        mixed_part = jnp.sum((gains * gains)[:, :, :, None] * weighted, axis=0)
        operated = collect(mixed_part) + lax.all_to_all(
            applied, "freq", split_axis=0, concat_axis=1, tiled=True
        )
        curve_sum = lax.psum(jnp.sum(direction * operated), ("tm", "freq", "dish"))
        step_size = energy_now / curve_sum
        estimate = estimate + step_size * direction
        residual = residual - step_size * operated
        if iteration + 1 < ITERS:
            scaled = precond * residual
            energy_next = energy_of(residual, scaled)
            direction = scaled + energy_next / energy_now * direction
            energy_now = energy_next
    return (estimate, residual)


def halves(value):
    high = value.astype(jnp.bfloat16).astype(jnp.float32)
    return high, value - high


def total(value):
    return jnp.sum(jnp.sum(value, axis=0, keepdims=True), axis=1, keepdims=True)


def kernel(
    sizes, time_hbm, pointing_hbm, coverage, noise_hbm, gains_hbm, prior_hbm,
    precond_hbm, x_out, r_out, time_data, noise, gains, prior, precond, rhs_sum, rhs_send, rhs_got, gain_send, gain_got, diag_wide, diag_send, diags,
    points, turned_points, tile_send, tiles_at, pre_got, mixing, model, state_x, state_r, state_u,
    state_p, state_w, pre, tile_p, same_half, other_half, u_send, field, back_send,
    back, fresh_send, fresh_got, curve_send, curve_got, end_send, end_recv, load_sems, setup_sems, leg_sems,
):
    tm, freq, dish = sizes
    group = tm * dish
    devices = group * freq
    dishes_dev, channels_dev, _ = time_data.shape
    blocks_dev = pointing_hbm.shape[0]
    blocks = tm * blocks_dev
    span_rows = blocks_dev * ROWS
    tiles_own = precond.shape[1] // LANES
    tiles = tiles_own * group
    pairs = devices // 2
    my_tm = lax.axis_index("tm")
    my_freq = lax.axis_index("freq")
    my_dish = lax.axis_index("dish")
    member = my_tm * dish + my_dish
    me = my_freq * group + member
    my_pair = lax.div(me, 2)
    my_half = lax.rem(me, 2)

    tm_at = [lax.rem(my_tm + step, tm) for step in range(tm)]
    freq_at = [lax.rem(my_freq + step, freq) for step in range(freq)]
    dish_at = [lax.rem(my_dish + step, dish) for step in range(dish)]
    steps = [
        (a, b, c) for b in range(freq) for a in range(tm) for c in range(dish)
    ]
    steps = sorted(steps[1:], key=lambda s: (-min(s[1], freq - s[1]), s))

    def index_of(step):
        a, b, c = step
        return freq_at[b] * group + tm_at[a] * dish + dish_at[c]

    def place(step):
        a, b, c = step
        return {"tm": tm_at[a], "freq": freq_at[b], "dish": dish_at[c]}

    def remote(src, dst, send, recv, step):
        return pltpu.make_async_remote_copy(
            src_ref=src, dst_ref=dst, send_sem=send, recv_sem=recv,
            device_id=place(step), device_id_type=MESH,
        )

    def wait_bytes(ref, sem):
        pltpu.make_async_copy(ref, ref, sem).wait()

    loads = [
        pltpu.make_async_copy(src, dst, load_sems.at[i])
        for i, (src, dst) in enumerate(
            [
                (noise_hbm, noise), (gains_hbm, gains), (time_hbm, time_data),
                (pointing_hbm, points.at[my_tm]), (precond_hbm, precond), (prior_hbm, prior),
            ]
        )
    ]
    for load in loads:
        load.start()
    barrier = pltpu.get_barrier_semaphore()
    for step in steps:
        pl.semaphore_signal(barrier, inc=1, device_id=place(step), device_id_type=MESH)

    at_row = lax.broadcasted_iota(jnp.int32, (LANES, LANES), 0)
    at_column = lax.broadcasted_iota(jnp.int32, (LANES, LANES), 1)
    reverse = jnp.where(at_row + at_column == LANES - 1, 1.0, 0.0).astype(jnp.bfloat16)

    rhs_sum[...] = jnp.zeros_like(rhs_sum)
    for load in loads[:3]:
        load.wait()

    def dish_step(d, carry):
        weight = gains[d]
        for b in range(blocks_dev):
            series = time_data[d, :, b * LANES:(b + 1) * LANES]
            term = lax.dot_general(
                noise[d], series, (((1,), (1,)), ((), ())),
                preferred_element_type=jnp.float32,
            )
            rhs_sum[b] += weight[b:b + 1, :] * term
        upside = jnp.dot(reverse, noise[d], preferred_element_type=jnp.float32)
        skewed = pltpu.roll(upside, 1, 1, stride=1, stride_axis=0)
        turned = jnp.dot(
            skewed.T.astype(jnp.bfloat16), reverse, preferred_element_type=jnp.float32
        )
        diag_wide[d] = turned[0:2 * BAND]
        return carry

    lax.fori_loop(0, dishes_dev, dish_step, 0)
    for b in range(blocks_dev):
        rhs_send[:, b] = rhs_sum[b].T.reshape(group, ROWS, LANES)
    for k in range(BAND + 1):
        diag_send[k] = diag_wide[:, k, :].astype(jnp.bfloat16)
    lane = lax.broadcasted_iota(jnp.int32, (dishes_dev, LANES), 1)
    slot = [
        jnp.logical_and(
            lane >= my_tm * span_rows + b * ROWS, lane < my_tm * span_rows + (b + 1) * ROWS
        )
        for b in range(blocks_dev)
    ]
    for t in range(group):
        column = jnp.zeros((dishes_dev, LANES), jnp.float32)
        for b in range(blocks_dev):
            turn = lax.rem(my_tm * span_rows + (b * ROWS - t * ROWS + LANES), LANES)
            column = jnp.where(slot[b], pltpu.roll(gains[:, b, :], turn, 1), column)
        gain_send[t] = column
    row = lax.broadcasted_iota(jnp.int32, (8, LANES), 0)
    tile_rows = jnp.zeros((8, LANES), jnp.int32)
    for b in range(blocks_dev):
        tile = lax.rem(my_tm * (tiles // tm) + coverage[b], tiles)
        tile_rows = jnp.where(row == b, tile, tile_rows)
    tile_send[...] = tile_rows

    for load in loads[3:]:
        load.wait()
    pl.semaphore_wait(barrier, devices - 1)

    group_steps = [step for step in steps if step[1] == 0]
    for step in group_steps:
        t = tm_at[step[0]] * dish + dish_at[step[2]]
        remote(
            rhs_send.at[t], rhs_got.at[member], setup_sems.at[0], setup_sems.at[1], step
        ).start()
        remote(
            precond.at[pl.ds(pl.multiple_of(t * ROWS, ROWS), ROWS), :], pre_got.at[member],
            setup_sems.at[2], setup_sems.at[3], step,
        ).start()
    for a in range(1, tm):
        step = (a, 0, 0)
        remote(tile_send, tiles_at.at[my_tm], setup_sems.at[6], setup_sems.at[7], step).start()
        remote(
            points.at[my_tm], points.at[my_tm], setup_sems.at[4], setup_sems.at[5], step
        ).start()
    for step in group_steps:
        t = tm_at[step[0]] * dish + dish_at[step[2]]
        remote(
            gain_send.at[t], gain_got.at[member], setup_sems.at[8], setup_sems.at[9], step
        ).start()
    for c in range(1, dish):
        remote(
            diag_send, diags.at[my_dish], setup_sems.at[10], setup_sems.at[11], (0, 0, c)
        ).start()
    rhs_got[member] = rhs_send[member]
    pre_got[member] = precond[pl.ds(pl.multiple_of(member * ROWS, ROWS), ROWS), :]
    tiles_at[my_tm] = tile_send[...]
    gain_got[member] = gain_send[member]
    diags[my_dish] = diag_send[...]

    channels = devices * ROWS
    rows_here = pairs * ROWS
    kept = prior[:, my_half].reshape(rows_here, channels)
    at_row = lax.broadcasted_iota(jnp.int32, (rows_here, channels), 0)
    at_column = lax.broadcasted_iota(jnp.int32, (rows_here, channels), 1)
    channel = (at_row // ROWS) * (2 * ROWS) + my_half * ROWS + at_row % ROWS
    kept = jnp.where(channel == at_column, 0.0, kept).astype(jnp.bfloat16)
    at_row = lax.broadcasted_iota(jnp.int32, (channels, rows_here), 0)
    at_column = lax.broadcasted_iota(jnp.int32, (channels, rows_here), 1)
    wanted = (at_column // ROWS) * (2 * ROWS) + at_column % ROWS
    for part, which in ((same_half, my_half), (other_half, 1 - my_half)):
        pick = jnp.where(at_row == wanted + which * ROWS, 1.0, 0.0).astype(jnp.bfloat16)
        part[...] = jnp.dot(kept, pick, preferred_element_type=jnp.float32).astype(jnp.bfloat16)
    own_rows = prior[my_pair, my_half]
    at_row = lax.broadcasted_iota(jnp.int32, (ROWS, channels), 0)
    at_column = lax.broadcasted_iota(jnp.int32, (ROWS, channels), 1)
    diagonal = jnp.sum(
        jnp.where(at_column == at_row + me * ROWS, own_rows, 0.0), axis=1, keepdims=True
    )

    def tile_row(b):
        one = tiles_at[b // blocks_dev, pl.ds(b % blocks_dev, 1), :]
        return jnp.broadcast_to(one, (ROWS, LANES))

    def back_project(rows):
        parts = [
            jnp.dot(
                rows[b * ROWS:(b + 1) * ROWS], points[b // blocks_dev, b % blocks_dev],
                preferred_element_type=jnp.float32,
            )
            for b in range(blocks)
        ]
        rows_at = [tile_row(b) for b in range(blocks)]
        summed = []
        for t in range(tiles):
            one = jnp.where(rows_at[0] == t, parts[0], 0.0)
            for b in range(1, blocks):
                one = one + jnp.where(rows_at[b] == t, parts[b], 0.0)
            summed.append(one)
        return summed

    wait_bytes(rhs_got.at[pl.ds(0, group - 1)], setup_sems.at[1])
    wait_bytes(pre_got.at[pl.ds(0, group - 1)], setup_sems.at[3])
    if tm > 1:
        wait_bytes(tiles_at.at[pl.ds(0, tm - 1)], setup_sems.at[7])
        wait_bytes(points.at[pl.ds(0, tm - 1)], setup_sems.at[5])
    rhs_list = []
    for k in range(tm):
        span = rhs_got[k * dish]
        for j in range(1, dish):
            span = span + rhs_got[k * dish + j]
        rhs_list.append(span.reshape(span_rows, LANES))
    rhs = jnp.concatenate(rhs_list, axis=0).astype(jnp.bfloat16)
    for t, one in enumerate(back_project(rhs)):
        first = (t % tiles_own) * LANES
        scale = pre_got[t // tiles_own, :, first:first + LANES]
        pre[t] = scale
        state_r[t] = one
        state_u[t] = scale * one
    zero = jnp.zeros((tiles, ROWS, LANES), jnp.float32)
    state_x[...] = zero
    state_p[...] = zero
    tile_p[...] = jnp.zeros_like(tile_p)

    like_steps = [step for step in steps if step[2] % 2 == 0]
    sibling = lax.rem(my_dish + 1, 2)
    sibling_place = {
        "tm": my_tm, "freq": my_freq, "dish": my_dish - my_half + sibling,
    }

    def send_like(src, dst, send, recv):
        for step in like_steps:
            remote(src.at[lax.div(index_of(step), 2)], dst, send, recv, step).start()

    def send_dots(src, dst, send, recv):
        for step in steps:
            remote(src, dst.at[me], send, recv, step).start()
        dst[me] = src[...]

    def sum_of(dots):
        return jnp.sum(jnp.sum(dots[...], axis=0), axis=1, keepdims=True)

    def begin():
        u_send[...] = state_u[...].astype(jnp.bfloat16)
        send_like(u_send, field.at[my_half, my_pair], leg_sems.at[0], leg_sems.at[1])
        field[my_half, my_pair] = u_send[my_pair]
        first = jnp.sum(state_r[...] * state_u[...], axis=0)
        fresh_send[...] = jnp.sum(first, axis=0, keepdims=True)
        send_dots(fresh_send, fresh_got, leg_sems.at[8], leg_sems.at[9])

    def mix_all():
        for b in range(blocks):
            one = points[b // blocks_dev, b % blocks_dev].astype(jnp.float32)
            turned_points[b] = one.T.astype(jnp.bfloat16)
        wait_bytes(gain_got.at[pl.ds(0, group - 1)], setup_sems.at[9])
        wait_bytes(diags.at[pl.ds(0, dish - 1)], setup_sems.at[11])
        gain_list = []
        for j in range(dish):
            column = gain_got[j]
            for k in range(1, tm):
                column = column + gain_got[k * dish + j]
            gain_list.append(column)
        gain = jnp.concatenate(gain_list, axis=0)
        high, low = halves(gain * gain)
        weights = jnp.concatenate([high, low], axis=0).T.astype(jnp.bfloat16)

        def mix(k, carry):
            one = [diags[j, k] for j in range(dish)]
            stacked = jnp.concatenate(one + one, axis=0)
            one = jnp.dot(weights, stacked, preferred_element_type=jnp.float32)
            mixing[BAND + k] = one
            mixing[BAND - k] = pltpu.roll(one, k, 1)
            return carry

        lax.fori_loop(0, BAND + 1, mix, 0)

    def iteration(index, energy_old):
        wait_bytes(field.at[0, pl.ds(0, pairs - 1)], leg_sems.at[1])
        forward = pltpu.make_async_remote_copy(
            src_ref=field.at[my_half], dst_ref=field.at[my_half],
            send_sem=leg_sems.at[2], recv_sem=leg_sems.at[3],
            device_id=sibling_place, device_id_type=MESH,
        )
        forward.start()
        wait_bytes(fresh_got.at[pl.ds(0, devices - 1)], leg_sems.at[9])
        energy = sum_of(fresh_got)
        beta = jnp.where(index == 0, 0.0, energy / energy_old)
        state_p[...] = state_u[...] + beta[None] * state_p[...]
        for b in range(blocks):
            at = tile_row(b)
            seen = jnp.where(at == 0, state_p[0], 0.0)
            for t in range(1, tiles):
                seen = seen + jnp.where(at == t, state_p[t], 0.0)
            model[b * ROWS:(b + 1) * ROWS] = jnp.dot(
                seen.astype(jnp.bfloat16), turned_points[b],
                preferred_element_type=jnp.float32,
            ).astype(jnp.bfloat16).astype(jnp.float32)

        forward.wait()
        mine = field[my_half].reshape(rows_here, LANES).astype(jnp.float32)
        mine = mine + beta * tile_p[my_half]
        tile_p[my_half] = mine
        theirs = field[1 - my_half].reshape(rows_here, LANES).astype(jnp.float32)
        theirs = theirs + beta * tile_p[1 - my_half]
        tile_p[1 - my_half] = theirs
        applied = jnp.dot(
            same_half[...], mine.astype(jnp.bfloat16), preferred_element_type=jnp.float32
        ) + jnp.dot(
            other_half[...], theirs.astype(jnp.bfloat16), preferred_element_type=jnp.float32
        )
        back_send[...] = applied.reshape(pairs, ROWS, LANES).astype(jnp.bfloat16)
        send_like(back_send, back.at[my_pair], leg_sems.at[4], leg_sems.at[5])
        back[my_pair] = back_send[my_pair]

        tod = model[...]
        mixed = mixing[BAND] * tod
        for k in range(DIAGS):
            if k != BAND:
                mixed = mixed + mixing[k] * pltpu.roll(tod, (BAND - k) % LANES, 1)
        curve = jnp.zeros((ROWS, LANES), jnp.float32)
        for t, one in enumerate(back_project(mixed.astype(jnp.bfloat16))):
            here = state_p[t]
            term = one + diagonal * here
            state_w[t] = term
            curve = curve + here * term
        curve_send[...] = jnp.sum(curve, axis=0, keepdims=True) + jnp.sum(
            applied * mine, axis=0, keepdims=True
        )
        send_dots(curve_send, curve_got, leg_sems.at[6], leg_sems.at[7])
        wait_bytes(back.at[pl.ds(0, pairs - 1)], leg_sems.at[5])
        wait_bytes(curve_got.at[pl.ds(0, devices - 1)], leg_sems.at[7])
        length = energy / sum_of(curve_got)
        for t in range(tiles):
            operated = state_w[t] + back[t].astype(jnp.float32)
            state_x[t] = state_x[t] + length * state_p[t]
            residual = state_r[t] - length * operated
            state_r[t] = residual
            state_u[t] = pre[t] * residual
        wait_bytes(u_send.at[pl.ds(0, pairs - 1)], leg_sems.at[0])
        wait_bytes(back_send.at[pl.ds(0, pairs - 1)], leg_sems.at[4])
        wait_bytes(curve_got.at[pl.ds(0, devices - 1)], leg_sems.at[6])
        wait_bytes(fresh_got.at[pl.ds(0, devices - 1)], leg_sems.at[8])
        return energy

    def later(index, energy):
        begin()
        return iteration(index, energy)

    begin()
    mix_all()
    energy = iteration(0, jnp.ones((1, 1), jnp.float32))
    lax.fori_loop(1, ITERS, later, energy)

    for t in range(tiles):
        first = (t % tiles_own) * LANES
        end_send[t // tiles_own, 0, :, first:first + LANES] = state_x[t]
        end_send[t // tiles_own, 1, :, first:first + LANES] = state_r[t]
    for step in group_steps:
        t = tm_at[step[0]] * dish + dish_at[step[2]]
        remote(
            end_send.at[t], end_recv.at[member], setup_sems.at[12], setup_sems.at[13], step
        ).start()
    end_recv[member] = end_send[member]
    wait_bytes(rhs_send.at[pl.ds(0, group - 1)], setup_sems.at[0])
    wait_bytes(pre_got.at[pl.ds(0, group - 1)], setup_sems.at[2])
    for a in range(1, tm):
        wait_bytes(points.at[0], setup_sems.at[4])
        wait_bytes(tile_send, setup_sems.at[6])
    wait_bytes(gain_send.at[pl.ds(0, group - 1)], setup_sems.at[8])
    wait_bytes(diags.at[pl.ds(0, dish - 1)], setup_sems.at[10])
    wait_bytes(end_recv.at[pl.ds(0, group - 1)], setup_sems.at[13])
    for t in range(group):
        x_out[t * ROWS:(t + 1) * ROWS] = end_recv[t, 0]
        r_out[t * ROWS:(t + 1) * ROWS] = end_recv[t, 1]
    wait_bytes(end_send.at[pl.ds(0, group - 1)], setup_sems.at[12])


def local_body(time_data, pointing, coverage, noise_inv, gains, prior_inv, precond):
    tm, freq, dish = (lax.axis_size(name) for name in ("tm", "freq", "dish"))
    group = tm * dish
    devices = group * freq
    pairs = devices // 2
    dishes_dev, channels_dev, _ = time_data.shape
    channels = prior_inv.shape[0]
    blocks_dev = pointing.shape[0]
    tiles_own = precond.shape[1] // LANES
    tiles = tiles_own * group

    f32, bf16 = jnp.float32, jnp.bfloat16
    state = pltpu.VMEM((tiles, ROWS, LANES), f32)
    half = pltpu.VMEM((pairs * ROWS, pairs * ROWS), bf16)
    leg = pltpu.VMEM((pairs, ROWS, LANES), bf16)
    end = pltpu.VMEM((group, 2, ROWS, tiles_own * LANES), f32)
    rhs = pltpu.VMEM((group, blocks_dev, ROWS, LANES), f32)
    gain = pltpu.VMEM((group, dishes_dev, LANES), f32)
    dots = pltpu.VMEM((1, LANES), f32)
    all_dots = pltpu.VMEM((devices, 1, LANES), f32)
    vmem = pl.BlockSpec(memory_space=pltpu.VMEM)
    hbm = pl.BlockSpec(memory_space=pl.ANY)
    smem = pl.BlockSpec(memory_space=pltpu.SMEM)
    shape = jax.ShapeDtypeStruct(precond.shape, f32)
    return pl.pallas_call(
        functools.partial(kernel, (tm, freq, dish)),
        out_shape=(shape, shape),
        in_specs=[hbm, hbm, smem, hbm, hbm, hbm, hbm],
        out_specs=(vmem, vmem),
        scratch_shapes=[
            pltpu.VMEM(time_data.shape, bf16),
            pltpu.VMEM(noise_inv.shape, bf16),
            pltpu.VMEM((dishes_dev, blocks_dev, channels_dev), f32),
            pltpu.VMEM((pairs, 2, ROWS, channels), f32),
            pltpu.VMEM(precond.shape, f32),
            pltpu.VMEM((blocks_dev, LANES, channels_dev), f32),
            rhs, rhs, gain, gain,
            pltpu.VMEM((dishes_dev, 2 * BAND, LANES), f32),
            pltpu.VMEM((BAND + 1, dishes_dev, LANES), bf16),
            pltpu.VMEM((dish, BAND + 1, dishes_dev, LANES), bf16),
            pltpu.VMEM((tm,) + pointing.shape, bf16),
            pltpu.VMEM((tm * blocks_dev, LANES, LANES), bf16),
            pltpu.VMEM((8, LANES), jnp.int32),
            pltpu.VMEM((tm, 8, LANES), jnp.int32),
            pltpu.VMEM((group, ROWS, tiles_own * LANES), f32),
            pltpu.VMEM((DIAGS, LANES, LANES), f32),
            pltpu.VMEM((LANES, LANES), f32),
            state, state, state, state, state, state,
            pltpu.VMEM((2, pairs * ROWS, LANES), f32),
            half, half, leg,
            pltpu.VMEM((2, pairs, ROWS, LANES), bf16),
            leg, leg,
            dots, all_dots, dots, all_dots, end, end,
            pltpu.SemaphoreType.DMA((6,)),
            pltpu.SemaphoreType.DMA((14,)),
            pltpu.SemaphoreType.DMA((10,)),
        ],
        compiler_params=pltpu.CompilerParams(
            collective_id=0, has_side_effects=True, vmem_limit_bytes=60 * 1024 * 1024
        ),
    )(
        time_data, pointing, coverage, noise_inv, gains.transpose(0, 2, 1),
        prior_inv.reshape(pairs, 2, ROWS, channels), precond,
    )


def body(time_data, pointing, coverage, noise_inv, gains, prior_inv, precond):
    group = lax.axis_size("tm") * lax.axis_size("dish")
    devices = group * lax.axis_size("freq")
    fits = (
        prior_inv.shape[0] == devices * ROWS
        and precond.shape[1] * group * 2 == devices * LANES
        and pointing.shape[0] * lax.axis_size("tm") * ROWS == LANES
        and time_data.shape[0] == ROWS
        and ROWS * lax.axis_size("dish") * 2 == LANES
        and time_data.shape[1] == LANES
    )
    run = local_body if fits else general_body
    return run(time_data, pointing, coverage, noise_inv, gains, prior_inv, precond)


def solution(mesh):
    return jax.shard_map(
        body,
        mesh=mesh,
        in_specs=(
            P("dish", "freq", "tm"),
            P("tm", None, None),
            P("tm"),
            P("dish", None, None),
            P("dish", "freq", "tm"),
            P(),
            P("freq", ("tm", "dish")),
        ),
        out_specs=(P("freq", ("tm", "dish")), P("freq", ("tm", "dish"))),
        check_vma=False,
    )
```

profile of v0, /device:TPU:0, one launch (start us, length us, event | category | flops | bytes accessed | tf_op | source)
XLA Modules:
  0.0 78.8 jit_solution(11204229075240204708)
XLA Ops:
  0.6 75.0 %shard_map.86 = (f32[128,256]{1,0:T(8,128)}, f32[128,256]{1,0:T(8,128)}) custom-call(bf16[16,128,512]{2,1,0:T(8,128)(2,1)} %time_hbm.1, bf16[4,128,128]{2,1,0:T(8,128)(2,1)} %pointing_hbm.1, s32[4]{0:T(128)} %coverage.1, bf16[16,128,128]{2,1,0:T(8,128)(2,1)} %noise_hbm.1, f32[16,4,128]{2,1,0:T(4,128)} %bitcast.3, f32[16,2,16,512]{3,2,1,0:T(8,128)} %bitcast.2, ...), custom_call_target="tpu_custom_call" | custom-call | tf_op jit(solution)/shard_map/pallas_call | solution.py:494
  75.7 1.6 %copy.11 = f32[128,256]{1,0:T(8,128)} copy(f32[128,256]{1,0:T(8,128)} %get-tuple-element.4) | data formatting | bytes 262144
  77.2 1.6 %copy.12 = f32[128,256]{1,0:T(8,128)} copy(f32[128,256]{1,0:T(8,128)} %get-tuple-element.5) | data formatting | bytes 262144
where the time goes:
time: 79 us; the launch traced here: 78.8 us
  Pallas kernels  75 us (95%)
  local copies, waits for them, and re-layouts  3.14 us (4%)
    pallas_call x1, Pallas kernels, local_body(): pl.pallas_call(functools.partial(kernel, (tm, freq, dish)), out_shape=(sh...  75 us
    unnamed x2, local copies, waits for them, and re-layouts  3.14 us

commit v1 on v0

--- a/solution.py
+++ b/solution.py
@@ -102,10 +102,10 @@
 
 def kernel(
     sizes, time_hbm, pointing_hbm, coverage, noise_hbm, gains_hbm, prior_hbm,
-    precond_hbm, x_out, r_out, time_data, noise, gains, prior, precond, rhs_sum, rhs_send, rhs_got, gain_send, gain_got, diag_wide, diag_send, diags,
+    precond_hbm, end_recv, time_data, noise, gains, prior, precond, rhs_sum, rhs_send, rhs_got, gain_send, gain_got, diag_wide, diag_send, diags,
     points, turned_points, tile_send, tiles_at, pre_got, mixing, model, state_x, state_r, state_u,
     state_p, state_w, pre, tile_p, same_half, other_half, u_send, field, back_send,
-    back, fresh_send, fresh_got, curve_send, curve_got, end_send, end_recv, load_sems, setup_sems, leg_sems,
+    back, fresh_send, fresh_got, curve_send, curve_got, end_send, load_sems, setup_sems, leg_sems,
 ):
     tm, freq, dish = sizes
     group = tm * dish
@@ -182,19 +182,57 @@
                 preferred_element_type=jnp.float32,
             )
             rhs_sum[b] += weight[b:b + 1, :] * term
+        return carry
+
+    def diagonal_step(d, carry):
         upside = jnp.dot(reverse, noise[d], preferred_element_type=jnp.float32)
         skewed = pltpu.roll(upside, 1, 1, stride=1, stride_axis=0)
         turned = jnp.dot(
-            skewed.T.astype(jnp.bfloat16), reverse, preferred_element_type=jnp.float32
-        )
-        diag_wide[d] = turned[0:2 * BAND]
+            skewed.T[0:2 * BAND].astype(jnp.bfloat16), reverse,
+            preferred_element_type=jnp.float32,
+        )
+        diag_wide[d] = turned
         return carry
 
-    lax.fori_loop(0, dishes_dev, dish_step, 0)
+    group_steps = [step for step in steps if step[1] == 0]
+    members = [tm_at[step[0]] * dish + dish_at[step[2]] for step in group_steps]
+    row = lax.broadcasted_iota(jnp.int32, (8, LANES), 0)
+    tile_rows = jnp.zeros((8, LANES), jnp.int32)
+    for b in range(blocks_dev):
+        tile = lax.rem(my_tm * (tiles // tm) + coverage[b], tiles)
+        tile_rows = jnp.where(row == b, tile, tile_rows)
+    tile_send[...] = tile_rows
+
+    lax.fori_loop(0, dishes_dev // 2, dish_step, 0, unroll=4)
+    for load in loads[3:]:
+        load.wait()
+    pl.semaphore_wait(barrier, devices - 1)
+    for a in range(1, tm):
+        step = (a, 0, 0)
+        remote(tile_send, tiles_at.at[my_tm], setup_sems.at[6], setup_sems.at[7], step).start()
+        remote(
+            points.at[my_tm], points.at[my_tm], setup_sems.at[4], setup_sems.at[5], step
+        ).start()
+    for step, t in zip(group_steps, members):
+        remote(
+            precond.at[pl.ds(pl.multiple_of(t * ROWS, ROWS), ROWS), :], pre_got.at[member],
+            setup_sems.at[2], setup_sems.at[3], step,
+        ).start()
+    lax.fori_loop(dishes_dev // 2, dishes_dev, dish_step, 0, unroll=4)
     for b in range(blocks_dev):
         rhs_send[:, b] = rhs_sum[b].T.reshape(group, ROWS, LANES)
+    for step, t in zip(group_steps, members):
+        remote(
+            rhs_send.at[t], rhs_got.at[member], setup_sems.at[0], setup_sems.at[1], step
+        ).start()
+
+    lax.fori_loop(0, dishes_dev, diagonal_step, 0, unroll=4)
     for k in range(BAND + 1):
         diag_send[k] = diag_wide[:, k, :].astype(jnp.bfloat16)
+    for c in range(1, dish):
+        remote(
+            diag_send, diags.at[my_dish], setup_sems.at[10], setup_sems.at[11], (0, 0, c)
+        ).start()
     lane = lax.broadcasted_iota(jnp.int32, (dishes_dev, LANES), 1)
     slot = [
         jnp.logical_and(
@@ -208,41 +246,10 @@
             turn = lax.rem(my_tm * span_rows + (b * ROWS - t * ROWS + LANES), LANES)
             column = jnp.where(slot[b], pltpu.roll(gains[:, b, :], turn, 1), column)
         gain_send[t] = column
-    row = lax.broadcasted_iota(jnp.int32, (8, LANES), 0)
-    tile_rows = jnp.zeros((8, LANES), jnp.int32)
-    for b in range(blocks_dev):
-        tile = lax.rem(my_tm * (tiles // tm) + coverage[b], tiles)
-        tile_rows = jnp.where(row == b, tile, tile_rows)
-    tile_send[...] = tile_rows
-
-    for load in loads[3:]:
-        load.wait()
-    pl.semaphore_wait(barrier, devices - 1)
-
-    group_steps = [step for step in steps if step[1] == 0]
-    for step in group_steps:
-        t = tm_at[step[0]] * dish + dish_at[step[2]]
-        remote(
-            rhs_send.at[t], rhs_got.at[member], setup_sems.at[0], setup_sems.at[1], step
-        ).start()
-        remote(
-            precond.at[pl.ds(pl.multiple_of(t * ROWS, ROWS), ROWS), :], pre_got.at[member],
-            setup_sems.at[2], setup_sems.at[3], step,
-        ).start()
-    for a in range(1, tm):
-        step = (a, 0, 0)
-        remote(tile_send, tiles_at.at[my_tm], setup_sems.at[6], setup_sems.at[7], step).start()
-        remote(
-            points.at[my_tm], points.at[my_tm], setup_sems.at[4], setup_sems.at[5], step
-        ).start()
     for step in group_steps:
         t = tm_at[step[0]] * dish + dish_at[step[2]]
         remote(
             gain_send.at[t], gain_got.at[member], setup_sems.at[8], setup_sems.at[9], step
-        ).start()
-    for c in range(1, dish):
-        remote(
-            diag_send, diags.at[my_dish], setup_sems.at[10], setup_sems.at[11], (0, 0, c)
         ).start()
     rhs_got[member] = rhs_send[member]
     pre_got[member] = precond[pl.ds(pl.multiple_of(member * ROWS, ROWS), ROWS), :]
@@ -356,15 +363,13 @@
         high, low = halves(gain * gain)
         weights = jnp.concatenate([high, low], axis=0).T.astype(jnp.bfloat16)
 
-        def mix(k, carry):
+        for k in range(BAND + 1):
             one = [diags[j, k] for j in range(dish)]
             stacked = jnp.concatenate(one + one, axis=0)
             one = jnp.dot(weights, stacked, preferred_element_type=jnp.float32)
             mixing[BAND + k] = one
-            mixing[BAND - k] = pltpu.roll(one, k, 1)
-            return carry
-
-        lax.fori_loop(0, BAND + 1, mix, 0)
+            if k > 0:
+                mixing[BAND - k] = pltpu.roll(one, k, 1)
 
     def iteration(index, energy_old):
         wait_bytes(field.at[0, pl.ds(0, pairs - 1)], leg_sems.at[1])
@@ -461,10 +466,13 @@
     wait_bytes(gain_send.at[pl.ds(0, group - 1)], setup_sems.at[8])
     wait_bytes(diags.at[pl.ds(0, dish - 1)], setup_sems.at[10])
     wait_bytes(end_recv.at[pl.ds(0, group - 1)], setup_sems.at[13])
-    for t in range(group):
-        x_out[t * ROWS:(t + 1) * ROWS] = end_recv[t, 0]
-        r_out[t * ROWS:(t + 1) * ROWS] = end_recv[t, 1]
     wait_bytes(end_send.at[pl.ds(0, group - 1)], setup_sems.at[12])
+
+
+def spread(ends, x_out, r_out):
+    for t in range(ends.shape[0]):
+        x_out[t * ROWS:(t + 1) * ROWS] = ends[t, 0]
+        r_out[t * ROWS:(t + 1) * ROWS] = ends[t, 1]
 
 
 def local_body(time_data, pointing, coverage, noise_inv, gains, prior_inv, precond):
@@ -491,11 +499,11 @@
     hbm = pl.BlockSpec(memory_space=pl.ANY)
     smem = pl.BlockSpec(memory_space=pltpu.SMEM)
     shape = jax.ShapeDtypeStruct(precond.shape, f32)
-    return pl.pallas_call(
+    ends = pl.pallas_call(
         functools.partial(kernel, (tm, freq, dish)),
-        out_shape=(shape, shape),
+        out_shape=jax.ShapeDtypeStruct((group, 2, ROWS, tiles_own * LANES), f32),
         in_specs=[hbm, hbm, smem, hbm, hbm, hbm, hbm],
-        out_specs=(vmem, vmem),
+        out_specs=vmem,
         scratch_shapes=[
             pltpu.VMEM(time_data.shape, bf16),
             pltpu.VMEM(noise_inv.shape, bf16),
@@ -519,7 +527,7 @@
             half, half, leg,
             pltpu.VMEM((2, pairs, ROWS, LANES), bf16),
             leg, leg,
-            dots, all_dots, dots, all_dots, end, end,
+            dots, all_dots, dots, all_dots, end,
             pltpu.SemaphoreType.DMA((6,)),
             pltpu.SemaphoreType.DMA((14,)),
             pltpu.SemaphoreType.DMA((10,)),
@@ -531,6 +539,9 @@
         time_data, pointing, coverage, noise_inv, gains.transpose(0, 2, 1),
         prior_inv.reshape(pairs, 2, ROWS, channels), precond,
     )
+    return pl.pallas_call(
+        spread, out_shape=(shape, shape), in_specs=[vmem], out_specs=(vmem, vmem)
+    )(ends)
 
 
 def body(time_data, pointing, coverage, noise_inv, gains, prior_inv, precond):

time: 79 us -> 71.2 us (0.901)
  Pallas kernels: 75 us -> 70.3 us
  local copies, waits for them, and re-layouts: 3.14 us -> 0 us
    pallas_call x1 -> x2, Pallas kernels: 75 us -> 70.3 us  [the longest x1 68.7 us: local_body(): pl.pallas_call(functools.partial(kernel, (tm, freq, dish)), out_shape=jax...]
    unnamed x2 -> x0, local copies, waits for them, and re-layouts: 3.14 us -> none
where the time goes in v1:
time: 71.2 us; the launch traced here: 71 us
  Pallas kernels  70.3 us (99%)
    pallas_call x1, Pallas kernels, local_body(): pl.pallas_call(functools.partial(kernel, (tm, freq, dish)), out_shape=jax...  68.7 us
    pallas_call x1, Pallas kernels, local_body(): pl.pallas_call(spread, out_shape=(shape, shape), in_specs=[vmem], out_spe...  1.67 us

profile of v1, /device:TPU:0, one launch (start us, length us, event | category | flops | bytes accessed | tf_op | source)
XLA Modules:
  0.0 71.0 jit_solution(3657778301544552611)
XLA Ops:
  0.6 68.7 %shard_map.86.ends = f32[8,2,16,256]{3,2,1,0:T(8,128)} custom-call(bf16[16,128,512]{2,1,0:T(8,128)(2,1)} %time_hbm.1, bf16[4,128,128]{2,1,0:T(8,128)(2,1)} %pointing_hbm.1, s32[4]{0:T(128)} %coverage.1, bf16[16,128,128]{2,1,0:T(8,128)(2,1)} %noise_hbm.1, f32[16,4,128]{2,1,0:T(4,128)} %bitcast.3, f32[16,2,16,512]{3,2,1,0:T(8,128)} %bitcast.2, ...), custom_call_target="tpu_custom_call" | custom-call | tf_op jit(solution)/shard_map/pallas_call | solution.py:502
  69.3 1.7 %shard_map.87 = (f32[128,256]{1,0:T(8,128)}, f32[128,256]{1,0:T(8,128)}) custom-call(f32[8,2,16,256]{3,2,1,0:T(8,128)} %shard_map.86.ends), custom_call_target="tpu_custom_call" | custom-call | tf_op jit(solution)/shard_map/pallas_call | solution.py:542

commit v2 on v1

--- a/solution.py
+++ b/solution.py
@@ -105,7 +105,7 @@
     precond_hbm, end_recv, time_data, noise, gains, prior, precond, rhs_sum, rhs_send, rhs_got, gain_send, gain_got, diag_wide, diag_send, diags,
     points, turned_points, tile_send, tiles_at, pre_got, mixing, model, state_x, state_r, state_u,
     state_p, state_w, pre, tile_p, same_half, other_half, u_send, field, back_send,
-    back, fresh_send, fresh_got, curve_send, curve_got, end_send, load_sems, setup_sems, leg_sems,
+    back, fresh_send, fresh_got, curve_send, curve_got, early_send, early_got, end_send, load_sems, setup_sems, leg_sems,
 ):
     tm, freq, dish = sizes
     group = tm * dish
@@ -259,17 +259,6 @@
 
     channels = devices * ROWS
     rows_here = pairs * ROWS
-    kept = prior[:, my_half].reshape(rows_here, channels)
-    at_row = lax.broadcasted_iota(jnp.int32, (rows_here, channels), 0)
-    at_column = lax.broadcasted_iota(jnp.int32, (rows_here, channels), 1)
-    channel = (at_row // ROWS) * (2 * ROWS) + my_half * ROWS + at_row % ROWS
-    kept = jnp.where(channel == at_column, 0.0, kept).astype(jnp.bfloat16)
-    at_row = lax.broadcasted_iota(jnp.int32, (channels, rows_here), 0)
-    at_column = lax.broadcasted_iota(jnp.int32, (channels, rows_here), 1)
-    wanted = (at_column // ROWS) * (2 * ROWS) + at_column % ROWS
-    for part, which in ((same_half, my_half), (other_half, 1 - my_half)):
-        pick = jnp.where(at_row == wanted + which * ROWS, 1.0, 0.0).astype(jnp.bfloat16)
-        part[...] = jnp.dot(kept, pick, preferred_element_type=jnp.float32).astype(jnp.bfloat16)
     own_rows = prior[my_pair, my_half]
     at_row = lax.broadcasted_iota(jnp.int32, (ROWS, channels), 0)
     at_column = lax.broadcasted_iota(jnp.int32, (ROWS, channels), 1)
@@ -347,6 +336,19 @@
         fresh_send[...] = jnp.sum(first, axis=0, keepdims=True)
         send_dots(fresh_send, fresh_got, leg_sems.at[8], leg_sems.at[9])
 
+    def order_prior():
+        kept = prior[:, my_half].reshape(rows_here, channels)
+        at_row = lax.broadcasted_iota(jnp.int32, (rows_here, channels), 0)
+        at_column = lax.broadcasted_iota(jnp.int32, (rows_here, channels), 1)
+        channel = (at_row // ROWS) * (2 * ROWS) + my_half * ROWS + at_row % ROWS
+        kept = jnp.where(channel == at_column, 0.0, kept).astype(jnp.bfloat16)
+        at_row = lax.broadcasted_iota(jnp.int32, (channels, rows_here), 0)
+        at_column = lax.broadcasted_iota(jnp.int32, (channels, rows_here), 1)
+        wanted = (at_column // ROWS) * (2 * ROWS) + at_column % ROWS
+        for part, which in ((same_half, my_half), (other_half, 1 - my_half)):
+            pick = jnp.where(at_row == wanted + which * ROWS, 1.0, 0.0).astype(jnp.bfloat16)
+            part[...] = jnp.dot(kept, pick, preferred_element_type=jnp.float32).astype(jnp.bfloat16)
+
     def mix_all():
         for b in range(blocks):
             one = points[b // blocks_dev, b % blocks_dev].astype(jnp.float32)
@@ -371,7 +373,7 @@
             if k > 0:
                 mixing[BAND - k] = pltpu.roll(one, k, 1)
 
-    def iteration(index, energy_old):
+    def iteration(index, energy_old, last=False):
         wait_bytes(field.at[0, pl.ds(0, pairs - 1)], leg_sems.at[1])
         forward = pltpu.make_async_remote_copy(
             src_ref=field.at[my_half], dst_ref=field.at[my_half],
@@ -393,6 +395,12 @@
                 preferred_element_type=jnp.float32,
             ).astype(jnp.bfloat16).astype(jnp.float32)
 
+        tod = model[...]
+        mixed = mixing[BAND] * tod
+        for k in range(DIAGS):
+            if k != BAND:
+                mixed = mixed + mixing[k] * pltpu.roll(tod, (BAND - k) % LANES, 1)
+
         forward.wait()
         mine = field[my_half].reshape(rows_here, LANES).astype(jnp.float32)
         mine = mine + beta * tile_p[my_half]
@@ -409,11 +417,6 @@
         send_like(back_send, back.at[my_pair], leg_sems.at[4], leg_sems.at[5])
         back[my_pair] = back_send[my_pair]
 
-        tod = model[...]
-        mixed = mixing[BAND] * tod
-        for k in range(DIAGS):
-            if k != BAND:
-                mixed = mixed + mixing[k] * pltpu.roll(tod, (BAND - k) % LANES, 1)
         curve = jnp.zeros((ROWS, LANES), jnp.float32)
         for t, one in enumerate(back_project(mixed.astype(jnp.bfloat16))):
             here = state_p[t]
@@ -424,40 +427,59 @@
             applied * mine, axis=0, keepdims=True
         )
         send_dots(curve_send, curve_got, leg_sems.at[6], leg_sems.at[7])
+        if last:
+            for t in range(tiles):
+                first = (t % tiles_own) * LANES
+                early_send[t // tiles_own, 0, :, first:first + LANES] = state_x[t]
+                early_send[t // tiles_own, 1, :, first:first + LANES] = state_p[t]
+            for step, t in zip(group_steps, members):
+                remote(
+                    early_send.at[t], early_got.at[member], setup_sems.at[14],
+                    setup_sems.at[15], step,
+                ).start()
+            early_got[member] = early_send[member]
         wait_bytes(back.at[pl.ds(0, pairs - 1)], leg_sems.at[5])
         wait_bytes(curve_got.at[pl.ds(0, devices - 1)], leg_sems.at[7])
         length = energy / sum_of(curve_got)
         for t in range(tiles):
             operated = state_w[t] + back[t].astype(jnp.float32)
-            state_x[t] = state_x[t] + length * state_p[t]
             residual = state_r[t] - length * operated
-            state_r[t] = residual
-            state_u[t] = pre[t] * residual
+            if last:
+                first = (t % tiles_own) * LANES
+                end_send[t // tiles_own, :, first:first + LANES] = residual
+            else:
+                state_x[t] = state_x[t] + length * state_p[t]
+                state_r[t] = residual
+                state_u[t] = pre[t] * residual
+        if last:
+            for step, t in zip(group_steps, members):
+                remote(
+                    end_send.at[t], end_recv.at[member, 1], setup_sems.at[12],
+                    setup_sems.at[13], step,
+                ).start()
+            end_recv[member, 1] = end_send[member]
         wait_bytes(u_send.at[pl.ds(0, pairs - 1)], leg_sems.at[0])
         wait_bytes(back_send.at[pl.ds(0, pairs - 1)], leg_sems.at[4])
         wait_bytes(curve_got.at[pl.ds(0, devices - 1)], leg_sems.at[6])
         wait_bytes(fresh_got.at[pl.ds(0, devices - 1)], leg_sems.at[8])
-        return energy
+        return length if last else energy
 
     def later(index, energy):
         begin()
         return iteration(index, energy)
 
     begin()
+    order_prior()
     mix_all()
     energy = iteration(0, jnp.ones((1, 1), jnp.float32))
-    lax.fori_loop(1, ITERS, later, energy)
-
-    for t in range(tiles):
-        first = (t % tiles_own) * LANES
-        end_send[t // tiles_own, 0, :, first:first + LANES] = state_x[t]
-        end_send[t // tiles_own, 1, :, first:first + LANES] = state_r[t]
-    for step in group_steps:
-        t = tm_at[step[0]] * dish + dish_at[step[2]]
-        remote(
-            end_send.at[t], end_recv.at[member], setup_sems.at[12], setup_sems.at[13], step
-        ).start()
-    end_recv[member] = end_send[member]
+    energy = lax.fori_loop(1, ITERS - 1, later, energy)
+    begin()
+    length = iteration(ITERS - 1, energy, last=True)
+
+    wait_bytes(early_got.at[pl.ds(0, group - 1)], setup_sems.at[15])
+    for t in range(group):
+        end_recv[t, 0] = early_got[t, 0] + length * early_got[t, 1]
+    wait_bytes(early_send.at[pl.ds(0, group - 1)], setup_sems.at[14])
     wait_bytes(rhs_send.at[pl.ds(0, group - 1)], setup_sems.at[0])
     wait_bytes(pre_got.at[pl.ds(0, group - 1)], setup_sems.at[2])
     for a in range(1, tm):
@@ -465,14 +487,22 @@
         wait_bytes(tile_send, setup_sems.at[6])
     wait_bytes(gain_send.at[pl.ds(0, group - 1)], setup_sems.at[8])
     wait_bytes(diags.at[pl.ds(0, dish - 1)], setup_sems.at[10])
-    wait_bytes(end_recv.at[pl.ds(0, group - 1)], setup_sems.at[13])
+    wait_bytes(end_send.at[pl.ds(0, group - 1)], setup_sems.at[13])
     wait_bytes(end_send.at[pl.ds(0, group - 1)], setup_sems.at[12])
 
 
-def spread(ends, x_out, r_out):
-    for t in range(ends.shape[0]):
-        x_out[t * ROWS:(t + 1) * ROWS] = ends[t, 0]
-        r_out[t * ROWS:(t + 1) * ROWS] = ends[t, 1]
+def spread(ends, x_out, r_out, sems):
+    copies = [
+        pltpu.make_async_copy(
+            ends.at[t, i], out.at[pl.ds(t * ROWS, ROWS), :], sems.at[t, i]
+        )
+        for t in range(ends.shape[0])
+        for i, out in enumerate((x_out, r_out))
+    ]
+    for copy in copies:
+        copy.start()
+    for copy in copies:
+        copy.wait()
 
 
 def local_body(time_data, pointing, coverage, noise_inv, gains, prior_inv, precond):
@@ -527,9 +557,10 @@
             half, half, leg,
             pltpu.VMEM((2, pairs, ROWS, LANES), bf16),
             leg, leg,
-            dots, all_dots, dots, all_dots, end,
+            dots, all_dots, dots, all_dots, end, end,
+            pltpu.VMEM((group, ROWS, tiles_own * LANES), f32),
             pltpu.SemaphoreType.DMA((6,)),
-            pltpu.SemaphoreType.DMA((14,)),
+            pltpu.SemaphoreType.DMA((16,)),
             pltpu.SemaphoreType.DMA((10,)),
         ],
         compiler_params=pltpu.CompilerParams(
@@ -540,7 +571,12 @@
         prior_inv.reshape(pairs, 2, ROWS, channels), precond,
     )
     return pl.pallas_call(
-        spread, out_shape=(shape, shape), in_specs=[vmem], out_specs=(vmem, vmem)
+        spread,
+        out_shape=(shape, shape),
+        in_specs=[hbm],
+        out_specs=(hbm, hbm),
+        scratch_shapes=[pltpu.SemaphoreType.DMA((group, 2))],
+        compiler_params=pltpu.CompilerParams(vmem_limit_bytes=60 * 1024 * 1024),
     )(ends)
 
 

time: 71.2 us -> 77.3 us (1.086)
  Pallas kernels: 70.3 us -> 76.5 us
    pallas_call x1, Pallas kernels: 1.67 us -> 9.19 us  [local_body(): pl.pallas_call(spread, out_shape=(shape, shape), in_specs=[hbm], out_spec...]
    pallas_call x1, Pallas kernels: 68.7 us -> 67.3 us  [local_body(): pl.pallas_call(functools.partial(kernel, (tm, freq, dish)), out_shape=jax...]
where the time goes in v2:
time: 77.3 us; the launch traced here: 77.1 us
  Pallas kernels  76.5 us (99%)
    pallas_call x1, Pallas kernels, local_body(): pl.pallas_call(functools.partial(kernel, (tm, freq, dish)), out_shape=jax...  67.3 us
    pallas_call x1, Pallas kernels, local_body(): pl.pallas_call(spread, out_shape=(shape, shape), in_specs=[hbm], out_spec...  9.19 us

profile of v2, /device:TPU:0, one launch (start us, length us, event | category | flops | bytes accessed | tf_op | source)
XLA Modules:
  0.0 77.1 jit_solution(18256797585715681538)
XLA Ops:
  0.6 67.3 %shard_map.86.ends = f32[8,2,16,256]{3,2,1,0:T(8,128)} custom-call(bf16[16,128,512]{2,1,0:T(8,128)(2,1)} %time_hbm.1, bf16[4,128,128]{2,1,0:T(8,128)(2,1)} %pointing_hbm.1, s32[4]{0:T(128)} %coverage.1, bf16[16,128,128]{2,1,0:T(8,128)(2,1)} %noise_hbm.1, f32[16,4,128]{2,1,0:T(4,128)} %bitcast.3, f32[16,2,16,512]{3,2,1,0:T(8,128)} %bitcast.2, ...), custom_call_target="tpu_custom_call" | custom-call | tf_op jit(solution)/shard_map/pallas_call | solution.py:532
  67.9 9.2 %shard_map.87 = (f32[128,256]{1,0:T(8,128)}, f32[128,256]{1,0:T(8,128)}) custom-call(f32[8,2,16,256]{3,2,1,0:T(8,128)} %shard_map.86.ends), custom_call_target="tpu_custom_call" | custom-call | tf_op jit(solution)/shard_map/pallas_call | solution.py:573

commit v3 on v2

--- a/solution.py
+++ b/solution.py
@@ -491,18 +491,10 @@
     wait_bytes(end_send.at[pl.ds(0, group - 1)], setup_sems.at[12])
 
 
-def spread(ends, x_out, r_out, sems):
-    copies = [
-        pltpu.make_async_copy(
-            ends.at[t, i], out.at[pl.ds(t * ROWS, ROWS), :], sems.at[t, i]
-        )
-        for t in range(ends.shape[0])
-        for i, out in enumerate((x_out, r_out))
-    ]
-    for copy in copies:
-        copy.start()
-    for copy in copies:
-        copy.wait()
+def spread(ends, x_out, r_out):
+    for t in range(ends.shape[0]):
+        x_out[t * ROWS:(t + 1) * ROWS] = ends[t, 0]
+        r_out[t * ROWS:(t + 1) * ROWS] = ends[t, 1]
 
 
 def local_body(time_data, pointing, coverage, noise_inv, gains, prior_inv, precond):
@@ -571,12 +563,7 @@
         prior_inv.reshape(pairs, 2, ROWS, channels), precond,
     )
     return pl.pallas_call(
-        spread,
-        out_shape=(shape, shape),
-        in_specs=[hbm],
-        out_specs=(hbm, hbm),
-        scratch_shapes=[pltpu.SemaphoreType.DMA((group, 2))],
-        compiler_params=pltpu.CompilerParams(vmem_limit_bytes=60 * 1024 * 1024),
+        spread, out_shape=(shape, shape), in_specs=[vmem], out_specs=(vmem, vmem)
     )(ends)
 
 

time: 77.3 us -> 69.8 us (0.903)
  Pallas kernels: 76.5 us -> 69 us
    pallas_call x1, Pallas kernels: 9.19 us -> 1.67 us  [local_body(): pl.pallas_call(spread, out_shape=(shape, shape), in_specs=[vmem], out_spe...]
where the time goes in v3:
time: 69.8 us; the launch traced here: 69.6 us
  Pallas kernels  69 us (99%)
    pallas_call x1, Pallas kernels, local_body(): pl.pallas_call(functools.partial(kernel, (tm, freq, dish)), out_shape=jax...  67.3 us
    pallas_call x1, Pallas kernels, local_body(): pl.pallas_call(spread, out_shape=(shape, shape), in_specs=[vmem], out_spe...  1.67 us

profile of v3, /device:TPU:0, one launch (start us, length us, event | category | flops | bytes accessed | tf_op | source)
XLA Modules:
  0.0 69.6 jit_solution(15162960507493364921)
XLA Ops:
  0.6 67.3 %shard_map.86.ends = f32[8,2,16,256]{3,2,1,0:T(8,128)} custom-call(bf16[16,128,512]{2,1,0:T(8,128)(2,1)} %time_hbm.1, bf16[4,128,128]{2,1,0:T(8,128)(2,1)} %pointing_hbm.1, s32[4]{0:T(128)} %coverage.1, bf16[16,128,128]{2,1,0:T(8,128)(2,1)} %noise_hbm.1, f32[16,4,128]{2,1,0:T(4,128)} %bitcast.3, f32[16,2,16,512]{3,2,1,0:T(8,128)} %bitcast.2, ...), custom_call_target="tpu_custom_call" | custom-call | tf_op jit(solution)/shard_map/pallas_call | solution.py:524
  67.9 1.7 %shard_map.87 = (f32[128,256]{1,0:T(8,128)}, f32[128,256]{1,0:T(8,128)}) custom-call(f32[8,2,16,256]{3,2,1,0:T(8,128)} %shard_map.86.ends), custom_call_target="tpu_custom_call" | custom-call | tf_op jit(solution)/shard_map/pallas_call | solution.py:565
